TPU v7x, 512 devices: a whole 4x4x16 slice. The times are simulated.
512 devices in a mesh: pipe: 8 (over x, core), dp: 64 (over y, z).
Axes of the slice: x: 4, y: 4, z: 16, core: 2. Of those that a mesh axis runs over, the one named last changes fastest.
Arguments:
- hidden_in: bfloat16 [8, 8192, 4096], P('pipe', 'dp'), may hold values from -20 to 20
- norm_gain: float32 [8, 2, 4096], P('pipe'), may hold values from 0.5 to 1.5
- self_kv: bfloat16 [8, 2, 8192, 1024], P('pipe', None, 'dp'), may hold values from -6 to 6
- prefix_kv: bfloat16 [8, 2, 8192, 1024], P('pipe', None, 'dp'), may hold values from -7 to 7
- partner_prefix: int32 [64], P('dp'), may hold values from 0 to 62, as said below
- resp_len: int32 [64], P('dp'), may hold values from 1 to 128, as said below
Outputs:
- hidden_out: bfloat16 [8, 8192, 4096], P('pipe', 'dp')
Inputs may be any that keep to these rules, and one draw needn't show every extreme that they name: 0 <= i - partner_prefix[i] <= 3 for every slot i, and a difference of 3 occurs in every draw. `resp_len`: the value 128 occurs in every draw.
All inputs are finite; a program needn't handle non-finite values.
Results may differ from a plain program's by a relative error of at most 0.012.
Values may be sent and summed in bfloat16 or wider, within the bound.
A program may use at most 64 MiB of HBM per device.

v0:
```python
import jax
import jax.numpy as jnp
from jax import lax
from jax.sharding import PartitionSpec as P

HEADS = 32
KV_HEADS = 4
HEAD_DIM = 128
LAYERS = 2
REACH = 4


def shifted(block, axis, distance):
    devices = range(lax.axis_size(axis))
    route = [(i - distance, i) for i in devices if i - distance in devices]
    return lax.ppermute(block, axis, route)


def from_behind(block, axis, distance):
    devices = range(lax.axis_size(axis))
    route = [((i - distance) % len(devices), i) for i in devices]
    return lax.ppermute(block, axis, route)


def fetch_prefix(block, offset):
    chosen = block
    for step in range(1, REACH):
        arrived = shifted(block, "dp", step)
        chosen = jnp.where(offset == step, arrived, chosen)
    return chosen


def one_layer(hidden, gain, own_kv, pre_kv, length):
    x = hidden.astype(jnp.float32)
    normed = x * lax.rsqrt(jnp.mean(x * x, axis=-1, keepdims=True) + 1e-05) * gain
    rows = x.shape[0]
    query = normed.astype(jnp.bfloat16).reshape(rows, KV_HEADS, HEADS // KV_HEADS, HEAD_DIM)
    keys_all = jnp.concatenate([pre_kv, own_kv], axis=0)
    span = keys_all.shape[0]
    keys = keys_all[:, : KV_HEADS * HEAD_DIM].reshape(span, KV_HEADS, HEAD_DIM)
    values = keys_all[:, KV_HEADS * HEAD_DIM :].reshape(span, KV_HEADS, HEAD_DIM)
    scores = jnp.einsum("rkgd,skd->kgrs", query, keys, preferred_element_type=jnp.float32)
    scores = scores / jnp.sqrt(jnp.float32(HEAD_DIM))
    row_pos = jnp.arange(rows)[:, None]
    key_pos = jnp.arange(span)[None, :] - pre_kv.shape[0]
    seen = (key_pos < 0) | (key_pos <= row_pos) & (key_pos < length)
    scores = jnp.where(seen, scores, jnp.float32(-1e30))
    top = jnp.max(scores, axis=-1, keepdims=True)
    expo = jnp.exp(scores - top)
    weights = (expo / jnp.sum(expo, axis=-1, keepdims=True)).astype(jnp.bfloat16)
    mixed = jnp.einsum("kgrs,skd->rkgd", weights, values, preferred_element_type=jnp.float32)
    return (x + mixed.reshape(rows, HEADS * HEAD_DIM)).astype(jnp.bfloat16)


def per_device(hidden_in, norm_gain, self_kv, prefix_kv, partner_prefix, resp_len):
    offset = lax.axis_index("dp") - partner_prefix[0]
    length = resp_len[0]
    hidden = hidden_in[0]
    for layer in range(LAYERS):
        fetched = fetch_prefix(prefix_kv[0, layer], offset)
        hidden = one_layer(hidden, norm_gain[0, layer], self_kv[0, layer], fetched, length)
    passed = from_behind(hidden, "pipe", 1)
    return passed[None]


def solution(mesh):
    return jax.shard_map(
        per_device,
        mesh=mesh,
        in_specs=(
            P("pipe", "dp", None),
            P("pipe", None, None),
            P("pipe", None, "dp", None),
            P("pipe", None, "dp", None),
            P("dp"),
            P("dp"),
        ),
        out_specs=P("pipe", "dp", None),
        check_vma=False,
    )
```

profile of v0, /device:TPU:24, one launch (start us, length us, event | category | flops | bytes accessed | tf_op | source)
XLA Modules:
  0.0 121.0 jit_solution(14875636263511194554)
XLA Ops:
  0.0 0.0 copy-start
  0.0 1.2 fusion.37
  1.2 0.9 copy.43
  2.0 3.8 %collective-permute-start.5 = (bf16[128,1024]{0,1:T(8,128)(2,1)}, bf16[128,1024]{0,1:T(8,128)(2,1)S(1)}, u32[]{:S(2)}, u32[]{:S(2)}) collective-permute-start(bf16[128,1024]{0,1:T(8,128)(2,1)} %bitcast.15), channel_id=1, source_target_pairs={{0,1},{1,2},{2,3},{3,4},{4,5},{5,6},{6,7},{7,8},{8,9},{9,10},{10,1... | collective-permute-start | bytes 786440 | tf_op jit(solution)/shard_map/ppermute | solution.py:16
  5.9 5.2 %collective-permute-start.4 = (bf16[128,1024]{0,1:T(8,128)(2,1)}, bf16[128,1024]{0,1:T(8,128)(2,1)}, u32[]{:S(2)}, u32[]{:S(2)}) collective-permute-start(bf16[128,1024]{0,1:T(8,128)(2,1)} %bitcast.15), channel_id=1, source_target_pairs={{0,2},{1,3},{2,4},{3,5},{4,6},{5,7},{6,8},{7,9},{8,10},{9,11},{10,... | collective-permute-start | bytes 786440 | tf_op jit(solution)/shard_map/ppermute | solution.py:16
  11.0 7.7 %collective-permute-start.3 = (bf16[128,1024]{0,1:T(8,128)(2,1)}, bf16[128,1024]{0,1:T(8,128)(2,1)}, u32[]{:S(2)}, u32[]{:S(2)}) collective-permute-start(bf16[128,1024]{0,1:T(8,128)(2,1)} %bitcast.15), channel_id=1, source_target_pairs={{0,3},{1,4},{2,5},{3,6},{4,7},{5,8},{6,9},{7,10},{8,11},{9,12},{10... | collective-permute-start | bytes 786440 | tf_op jit(solution)/shard_map/ppermute | solution.py:16
  18.8 0.8 copy.41
  19.6 3.8 %collective-permute-start.2 = (bf16[128,1024]{0,1:T(8,128)(2,1)}, bf16[128,1024]{0,1:T(8,128)(2,1)}, u32[]{:S(2)}, u32[]{:S(2)}) collective-permute-start(bf16[128,1024]{0,1:T(8,128)(2,1)} %bitcast.2), channel_id=1, source_target_pairs={{0,1},{1,2},{2,3},{3,4},{4,5},{5,6},{6,7},{7,8},{8,9},{9,10},{10,1... | collective-permute-start | bytes 786440 | tf_op jit(solution)/shard_map/ppermute | solution.py:16
  23.4 5.5 %collective-permute-start.1 = (bf16[128,1024]{0,1:T(8,128)(2,1)}, bf16[128,1024]{0,1:T(8,128)(2,1)}, u32[]{:S(2)}, u32[]{:S(2)}) collective-permute-start(bf16[128,1024]{0,1:T(8,128)(2,1)} %bitcast.2), channel_id=1, source_target_pairs={{0,2},{1,3},{2,4},{3,5},{4,6},{5,7},{6,8},{7,9},{8,10},{9,11},{10,... | collective-permute-start | bytes 786440 | tf_op jit(solution)/shard_map/ppermute | solution.py:16
  28.9 1.5 %fusion.8 = f32[128]{0:T(128)S(1)} fusion(bf16[1,128,4096]{2,1,0:T(8,128)(2,1)} %param.6), kind=kLoop, calls=%fused_computation.19 | loop fusion | flops 1572736 | bytes 1049088 | tf_op jit(solution)/shard_map/reduce_sum | solution.py:35
  30.5 0.9 fusion.38
  32.0 1.8 %fusion.36 = (bf16[1,1,128,1024]{3,2,1,0:T(8,128)(2,1)S(1)}, bf16[1,1,128,1024]{3,2,1,0:T(8,128)(2,1)}) fusion(bf16[1,2,128,1024]{3,2,1,0:T(8,128)(2,1)} %param.8), kind=kLoop, calls=%fused_computation.59 | loop fusion | bytes 1048576 | tf_op jit(solution)/shard_map/slice | solution.py:61
  33.8 0.0 collective-permute-done.5
  33.8 0.0 copy-start.1
  33.8 3.8 %collective-permute-start = (bf16[128,1024]{0,1:T(8,128)(2,1)}, bf16[128,1024]{0,1:T(8,128)(2,1)}, u32[]{:S(2)}, u32[]{:S(2)}) collective-permute-start(bf16[128,1024]{0,1:T(8,128)(2,1)} %bitcast.2), channel_id=1, source_target_pairs={{0,3},{1,4},{2,5},{3,6},{4,7},{5,8},{6,9},{7,10},{8,11},{9,12},{10... | collective-permute-start | bytes 786440 | tf_op jit(solution)/shard_map/ppermute | solution.py:16
  37.6 0.0 copy-done.1
  37.6 0.0 copy-done
  37.6 0.5 copy.18
  38.8 0.8 copy.42
  39.7 1.1 copy.44
  40.8 0.2 fusion.28
  41.0 0.0 collective-permute-done.4
  41.0 9.7 %collective-permute-done.3 = bf16[128,1024]{0,1:T(8,128)(2,1)} collective-permute-done((bf16[128,1024]{0,1:T(8,128)(2,1)}, bf16[128,1024]{0,1:T(8,128)(2,1)}, u32[]{:S(2)}, u32[]{:S(2)}) %collective-permute-start.3) | collective-permute-done | bytes 262176 | tf_op jit(solution)/shard_map/ppermute | solution.py:16
  50.7 4.6 %collective-permute-done.2 = bf16[128,1024]{0,1:T(8,128)(2,1)} collective-permute-done((bf16[128,1024]{0,1:T(8,128)(2,1)}, bf16[128,1024]{0,1:T(8,128)(2,1)}, u32[]{:S(2)}, u32[]{:S(2)}) %collective-permute-start.2) | collective-permute-done | bytes 262176 | tf_op jit(solution)/shard_map/ppermute | solution.py:16
  55.2 14.2 %collective-permute-done.1 = bf16[128,1024]{0,1:T(8,128)(2,1)} collective-permute-done((bf16[128,1024]{0,1:T(8,128)(2,1)}, bf16[128,1024]{0,1:T(8,128)(2,1)}, u32[]{:S(2)}, u32[]{:S(2)}) %collective-permute-start.1) | collective-permute-done | bytes 262176 | tf_op jit(solution)/shard_map/ppermute | solution.py:16
  69.4 14.2 %collective-permute-done = bf16[128,1024]{0,1:T(8,128)(2,1)} collective-permute-done((bf16[128,1024]{0,1:T(8,128)(2,1)}, bf16[128,1024]{0,1:T(8,128)(2,1)}, u32[]{:S(2)}, u32[]{:S(2)}) %collective-permute-start) | collective-permute-done | bytes 262176 | tf_op jit(solution)/shard_map/ppermute | solution.py:16
  83.6 1.9 %select_select_fusion = (bf16[128,1024]{0,1:T(8,128)(2,1)}, bf16[128,1024]{0,1:T(8,128)(2,1)S(1)}) fusion(bf16[128,1024]{0,1:T(8,128)(2,1)} %collective-permute-done.3, bf16[128,1024]{0,1:T(8,128)(2,1)} %collective-permute-done.4, bf16[128,1024]{0,1:T(8,128)(2,1)} %copy-done.1, pred[]{:T(512)S(6)} %eq.14, pred[]{:T(512)S(6)} %eq.13, pred[]{:T(512)S(6)} %eq.12, ...), kind=kLoop, calls=%fused_computation.45 | loop fusion | flops 786432 | bytes 2621443 | tf_op jit(solution)/shard_map/jit(_where)/select_n | solution.py:29
  85.5 1.0 pad_maximum_fusion.1
  86.5 1.4 %fusion.18 = f32[4,256,128,8]{2,1,3,0:T(8,128)S(1)} fusion(bf16[256,4,128,1]{0,2,3,1:T(8,128)(2,1)S(1)} %bitcast.87, f32[128,4,8,128]{0,3,2,1:T(8,128)S(1)} %bitcast.79, f32[4,8,128]{2,1,0:T(8,128)S(1)} %bitcast.91, f32[128]{0:T(128)S(1)} %add_rsqrt_fusion.1), kind=kOutput, calls=%fused_computation.31 | convolution fusion | flops 270008320 | bytes 6570496 | tf_op jit(solution)/shard_map/rkgd,skd->kgrs/dot_general | solution.py:42
  87.9 1.1 fusion.39
  89.1 2.3 %fusion.4 = (f32[128]{0:T(128)S(1)}, bf16[128,4,8,128]{0,3,2,1:T(8,128)(2,1)}, f32[4,128,8,128]{3,1,2,0:T(8,128)}) fusion(f32[128,4,8,128]{0,3,2,1:T(8,128)S(1)} %bitcast.80, bf16[256,4,128,1]{0,2,3,1:T(8,128)(2,1)S(1)} %bitcast.88, f32[4,8,128,256]{2,3,1,0:T(8,128)S(1)} %get-tuple-element.18, f32[4,8,128]{2,1,0:T(8,128)S(1)} %get-tuple-element.17), kind=kOutput, calls=%fused_computation.12 | convolution fusion | flops 273153920 | bytes 9716224 | tf_op jit(solution)/shard_map/kgrs,skd->rkgd/dot_general | solution.py:51
  91.4 1.9 %copy.22 = f32[128,4096]{1,0:T(8,128)S(1)} copy(f32[128,4096]{0,1:T(8,128)} %bitcast.81) | data formatting | bytes 4194304 | tf_op jit(solution)/shard_map/reshape | solution.py:52
  93.3 1.0 pad_maximum_fusion
  94.4 2.4 %fusion.19 = f32[4,256,128,8]{2,1,3,0:T(8,128)S(1)} fusion(bf16[256,4,128,1]{0,2,3,1:T(8,128)(2,1)S(1)} %bitcast.84, bf16[128,4,8,128]{0,3,2,1:T(8,128)(2,1)} %get-tuple-element.6, f32[4,8,128]{2,1,0:T(8,128)S(1)} %bitcast.90, f32[128]{0:T(128)S(1)} %add_rsqrt_fusion), kind=kOutput, calls=%fused_computation.32 | convolution fusion | flops 270532608 | bytes 5521920 | tf_op jit(solution)/shard_map/rkgd,skd->kgrs/dot_general | solution.py:42
  96.8 1.1 fusion.40
  97.9 1.8 %fusion.15 = f32[4,128,8,128]{3,1,2,0:T(8,128)} fusion(bf16[256,4,128,1]{0,2,3,1:T(8,128)(2,1)S(1)} %bitcast.89, f32[4,8,128,256]{2,3,1,0:T(8,128)S(1)} %get-tuple-element.21, f32[4,8,128]{2,1,0:T(8,128)S(1)} %get-tuple-element.20), kind=kOutput, calls=%fused_computation.28 | convolution fusion | flops 270532608 | bytes 6569984 | tf_op jit(solution)/shard_map/kgrs,skd->rkgd/dot_general | solution.py:51
  99.7 2.9 %copy.28 = f32[128,4096]{1,0:T(8,128)} copy(f32[128,4096]{0,1:T(8,128)} %bitcast.82) | data formatting | bytes 4194304 | tf_op jit(solution)/shard_map/reshape | solution.py:52
  102.6 1.9 %add_convert_fusion = bf16[128,4096]{1,0:T(8,128)(2,1)S(1)} fusion(f32[128,4096]{1,0:T(8,128)} %copy.28, f32[128,4096]{1,0:T(8,128)S(1)} %copy.22, bf16[1,128,4096]{2,1,0:T(8,128)(2,1)S(1)} %copy-done), kind=kLoop, calls=%fused_computation.21 | loop fusion | flops 3145728 | bytes 6291456 | tf_op jit(solution)/shard_map/convert_element_type | solution.py:52
  104.5 0.0 collective-permute-start.6
  104.6 15.4 %collective-permute-done.6 = bf16[128,4096]{1,0:T(8,128)(2,1)S(1)} collective-permute-done((bf16[128,4096]{1,0:T(8,128)(2,1)S(1)}, bf16[128,4096]{1,0:T(8,128)(2,1)S(1)}, u32[]{:S(2)}, u32[]{:S(2)}) %collective-permute-start.6) | collective-permute-done | bytes 1048608 | tf_op jit(solution)/shard_map/ppermute | solution.py:22
  120.0 1.0 copy.48
  (4 shorter events, 0.0 us)
Async XLA Ops:
  0.0 37.6 %copy-start = (bf16[1,128,4096]{2,1,0:T(8,128)(2,1)S(1)}, bf16[1,128,4096]{2,1,0:T(8,128)(2,1)}, u32[]{:S(2)}) copy-start(bf16[1,128,4096]{2,1,0:T(8,128)(2,1)} %param.6) | copy-start | bytes 3145732
  2.0 31.7 %collective-permute-start.5 = (bf16[128,1024]{0,1:T(8,128)(2,1)}, bf16[128,1024]{0,1:T(8,128)(2,1)S(1)}, u32[]{:S(2)}, u32[]{:S(2)}) collective-permute-start(bf16[128,1024]{0,1:T(8,128)(2,1)} %bitcast.15), channel_id=1, source_target_pairs={{0,1},{1,2},{2,3},{3,4},{4,5},{5,6},{6,7},{7,8},{8,9},{9,10},{10,1... | collective-permute-start | bytes 786440 | tf_op jit(solution)/shard_map/ppermute | solution.py:16
  5.9 35.1 %collective-permute-start.4 = (bf16[128,1024]{0,1:T(8,128)(2,1)}, bf16[128,1024]{0,1:T(8,128)(2,1)}, u32[]{:S(2)}, u32[]{:S(2)}) collective-permute-start(bf16[128,1024]{0,1:T(8,128)(2,1)} %bitcast.15), channel_id=1, source_target_pairs={{0,2},{1,3},{2,4},{3,5},{4,6},{5,7},{6,8},{7,9},{8,10},{9,11},{10,... | collective-permute-start | bytes 786440 | tf_op jit(solution)/shard_map/ppermute | solution.py:16
  11.0 39.6 %collective-permute-start.3 = (bf16[128,1024]{0,1:T(8,128)(2,1)}, bf16[128,1024]{0,1:T(8,128)(2,1)}, u32[]{:S(2)}, u32[]{:S(2)}) collective-permute-start(bf16[128,1024]{0,1:T(8,128)(2,1)} %bitcast.15), channel_id=1, source_target_pairs={{0,3},{1,4},{2,5},{3,6},{4,7},{5,8},{6,9},{7,10},{8,11},{9,12},{10... | collective-permute-start | bytes 786440 | tf_op jit(solution)/shard_map/ppermute | solution.py:16
  19.6 35.6 %collective-permute-start.2 = (bf16[128,1024]{0,1:T(8,128)(2,1)}, bf16[128,1024]{0,1:T(8,128)(2,1)}, u32[]{:S(2)}, u32[]{:S(2)}) collective-permute-start(bf16[128,1024]{0,1:T(8,128)(2,1)} %bitcast.2), channel_id=1, source_target_pairs={{0,1},{1,2},{2,3},{3,4},{4,5},{5,6},{6,7},{7,8},{8,9},{9,10},{10,1... | collective-permute-start | bytes 786440 | tf_op jit(solution)/shard_map/ppermute | solution.py:16
  23.4 46.0 %collective-permute-start.1 = (bf16[128,1024]{0,1:T(8,128)(2,1)}, bf16[128,1024]{0,1:T(8,128)(2,1)}, u32[]{:S(2)}, u32[]{:S(2)}) collective-permute-start(bf16[128,1024]{0,1:T(8,128)(2,1)} %bitcast.2), channel_id=1, source_target_pairs={{0,2},{1,3},{2,4},{3,5},{4,6},{5,7},{6,8},{7,9},{8,10},{9,11},{10,... | collective-permute-start | bytes 786440 | tf_op jit(solution)/shard_map/ppermute | solution.py:16
  33.8 3.9 %copy-start.1 = (bf16[128,1024]{0,1:T(8,128)(2,1)}, bf16[128,1024]{0,1:T(8,128)(2,1)S(1)}, u32[]{:S(2)}) copy-start(bf16[128,1024]{0,1:T(8,128)(2,1)S(1)} %collective-permute-done.5) | copy-start | bytes 786436
  33.8 49.8 %collective-permute-start = (bf16[128,1024]{0,1:T(8,128)(2,1)}, bf16[128,1024]{0,1:T(8,128)(2,1)}, u32[]{:S(2)}, u32[]{:S(2)}) collective-permute-start(bf16[128,1024]{0,1:T(8,128)(2,1)} %bitcast.2), channel_id=1, source_target_pairs={{0,3},{1,4},{2,5},{3,6},{4,7},{5,8},{6,9},{7,10},{8,11},{9,12},{10... | collective-permute-start | bytes 786440 | tf_op jit(solution)/shard_map/ppermute | solution.py:16
  104.5 15.4 %collective-permute-start.6 = (bf16[128,4096]{1,0:T(8,128)(2,1)S(1)}, bf16[128,4096]{1,0:T(8,128)(2,1)S(1)}, u32[]{:S(2)}, u32[]{:S(2)}) collective-permute-start(bf16[128,4096]{1,0:T(8,128)(2,1)S(1)} %add_convert_fusion), channel_id=1, source_target_pairs={{448,0},{0,64},{64,128},{128,192},{192,256},{256,320},{320,384},{3... | collective-permute-start | bytes 3145736 | tf_op jit(solution)/shard_map/ppermute | solution.py:22
where the time goes:
time: 122 us; the launch traced here: 121 us
  waiting for transfers between devices  58.1 us (48%)
  starting transfers between devices  29.9 us (25%)
  local copies, waits for them, and re-layouts  13.8 us (11%)
  other arithmetic  9.82 us (8%)
  matrix products  7.95 us (7%)
  between operations  1.48 us (1%)
    ppermute x6, waiting for transfers between devices, shifted(): return lax.ppermute(block, axis, route)  42.6 us
    ppermute x6, starting transfers between devices, shifted(): return lax.ppermute(block, axis, route)  29.9 us
    ppermute x1, waiting for transfers between devices, from_behind(): return lax.ppermute(block, axis, route)  15.4 us
    reshape x2, local copies, waits for them, and re-layouts, one_layer(): return (x + mixed.reshape(rows, HEADS * HEAD_DIM)).astype(jnp.bfloat16)  4.82 us
    unnamed x9, local copies, waits for them, and re-layouts  4.63 us
    dot_general x2, matrix products, one_layer(): jnp.einsum('kgrs,skd->rkgd', weights, values, preferred_element_type=jnp....  4.14 us
    dot_general x2, matrix products, one_layer(): jnp.einsum('rkgd,skd->kgrs', query, keys, preferred_element_type=jnp.floa...  3.81 us
  transfers between devices with their start and end apart: 7, of which 5 were waited for; matrix products, arithmetic and copies ran while one was open for 6% of the time, Pallas kernels for 0%

commit v1 on v0

v1 whole, which is shorter than its diff:
```python
import math

import jax
import jax.numpy as jnp
from jax import lax
from jax.experimental import pallas as pl
from jax.experimental.pallas import tpu as pltpu
from jax.sharding import PartitionSpec as P

HEADS = 32
KV_HEADS = 4
GROUP = HEADS // KV_HEADS
HEAD_DIM = 128
LAYERS = 2
REACH = 4
RESP = 128
WIN = HEADS * HEAD_DIM
KVW = 2 * KV_HEADS * HEAD_DIM
HALF = KVW // 2
PIECES = 2 * KV_HEADS
SCALE = math.log2(math.e) / math.sqrt(HEAD_DIM)
OUT_PARTS = 8
PART = WIN // OUT_PARTS
MESH = pl.DeviceIdType.MESH


def kernel(hid_ref, gain_ref, own_ref, pre_ref, partner, length, out_ref,
           h, q, own, gain, pre, kcat, vcat, bias, squares,
           load_sem, slot_sem, send_sem, recv_sem, out_send, out_recv):
    pipe, dp = lax.axis_index("pipe"), lax.axis_index("dp")
    sections, owners = lax.axis_size("pipe"), lax.axis_size("dp")
    right = (pipe, lax.rem(dp + 1, owners))
    left = (pipe, lax.rem(dp + owners - 1, owners))
    onward = (lax.rem(pipe + 1, sections), dp)
    back = (lax.rem(pipe + sections - 1, sections), dp)

    barrier = pltpu.get_barrier_semaphore()
    for device in (left, back):
        pl.semaphore_signal(barrier, inc=1, device_id=device, device_id_type=MESH)

    def column(piece):
        return (piece % 2) * HALF + (piece // 2) * HEAD_DIM

    def owned(layer, piece):
        return pre_ref.at[0, layer, :, pl.ds(column(piece), HEAD_DIM)]

    loads = [
        pltpu.make_async_copy(hid_ref.at[0], h, load_sem.at[0]),
        pltpu.make_async_copy(gain_ref.at[0], gain, load_sem.at[1]),
        pltpu.make_async_copy(own_ref.at[0], own, load_sem.at[2]),
    ]
    slots = [
        pltpu.make_async_copy(owned(layer, piece), pre.at[layer, piece, 0], slot_sem.at[layer, piece])
        for layer in range(LAYERS)
        for piece in range(PIECES)
    ]
    for copy in loads:
        copy.start()
    pl.semaphore_wait(barrier, 2)

    def hop(layer, piece, step):
        source = owned(layer, piece) if step == 1 else pre.at[layer, piece, step - 1]
        return pltpu.make_async_remote_copy(
            src_ref=source,
            dst_ref=pre.at[layer, piece, step],
            send_sem=send_sem.at[layer, piece, step - 1],
            recv_sem=recv_sem.at[layer, piece, step - 1],
            device_id=right,
            device_id_type=MESH,
        )

    def forward(layer, pieces, step):
        for piece in pieces:
            if step > 1:
                hop(layer, piece, step - 1).wait_recv()
            hop(layer, piece, step).start()

    def handed(part):
        columns = pl.ds(part * PART, PART)
        return pltpu.make_async_remote_copy(
            src_ref=h.at[:, columns],
            dst_ref=out_ref.at[0, :, columns],
            send_sem=out_send.at[part],
            recv_sem=out_recv.at[part],
            device_id=onward,
            device_id_type=MESH,
        )

    def head_columns(head):
        return pl.ds(pl.multiple_of(head * HEAD_DIM, HEAD_DIM), HEAD_DIM)

    def add_squares():
        squares[...] = jnp.zeros_like(squares)

        @pl.loop(0, HEADS // GROUP)
        def _(group):
            summed = squares[...]
            for within in range(GROUP):
                x = h[:, head_columns(group * GROUP + within)].astype(jnp.float32)
                summed = summed + x * x
            squares[...] = summed

    def queries(layer):
        mean = jnp.sum(squares[...], axis=-1, keepdims=True) * (1.0 / WIN)
        factor = jnp.broadcast_to(lax.rsqrt(mean + 1e-05), (RESP, HEAD_DIM))

        @pl.loop(0, HEADS // GROUP)
        def _(group):
            for within in range(GROUP):
                columns = head_columns(group * GROUP + within)
                x = h[:, columns].astype(jnp.float32)
                q[:, columns] = (x * factor * gain[pl.ds(layer, 1), columns]).astype(jnp.bfloat16)

    def chosen(layer, piece):
        offset = dp - partner[0]
        block = pre[layer, piece, 0]
        for step in range(1, REACH):
            block = jnp.where(offset == step, pre[layer, piece, step], block)
        return block

    def mix(columns):
        scores = lax.dot_general(
            q[:, columns], kcat[...], (((1,), (1,)), ((), ())), preferred_element_type=jnp.float32
        )
        scores = scores * SCALE + bias[...]
        top = jnp.max(scores, axis=-1, keepdims=True)
        expo = jnp.exp2(scores - top).astype(jnp.bfloat16)
        mixed = jnp.dot(expo, vcat[...], preferred_element_type=jnp.float32)
        return mixed[:, :HEAD_DIM] / mixed[:, HEAD_DIM:]

    def attend(layer, group, first, last):
        heads = [pl.ds((group * GROUP + within) * HEAD_DIM, HEAD_DIM) for within in range(first, last)]
        mixes = [mix(columns) for columns in heads]
        summed = squares[...] if layer + 1 < LAYERS else None
        for columns, mixed in zip(heads, mixes):
            total = (h[:, columns].astype(jnp.float32) + mixed).astype(jnp.bfloat16)
            h[:, columns] = total
            if layer + 1 < LAYERS:
                x = total.astype(jnp.float32)
                summed = summed + x * x
        if layer + 1 < LAYERS:
            squares[...] = summed

    def settle(layer, group):
        for piece in (2 * group, 2 * group + 1):
            hop(layer, piece, REACH - 1).wait_recv()
            slots[layer * PIECES + piece].wait()
        kcat[pl.ds(0, RESP), :] = chosen(layer, 2 * group)
        kcat[pl.ds(RESP, RESP), :] = own[layer, :, pl.ds(group * HEAD_DIM, HEAD_DIM)]
        vcat[pl.ds(0, RESP), pl.ds(0, HEAD_DIM)] = chosen(layer, 2 * group + 1)
        vcat[pl.ds(RESP, RESP), pl.ds(0, HEAD_DIM)] = own[layer, :, pl.ds(HALF + group * HEAD_DIM, HEAD_DIM)]

    every = range(PIECES)
    forward(0, every, 1)
    for copy in slots:
        copy.start()
    vcat[:, pl.ds(HEAD_DIM, HEAD_DIM)] = jnp.ones((2 * RESP, HEAD_DIM), jnp.bfloat16)
    for copy in loads:
        copy.wait()
    row = lax.broadcasted_iota(jnp.int32, (RESP, RESP), 0)
    key = lax.broadcasted_iota(jnp.int32, (RESP, RESP), 1)
    seen = (key <= row) & (key < length[0])
    bias[:, pl.ds(0, RESP)] = jnp.zeros((RESP, RESP), jnp.float32)
    bias[:, pl.ds(RESP, RESP)] = jnp.where(seen, 0.0, -1e30)
    forward(0, every[:4], 2)
    add_squares()
    queries(0)
    squares[...] = jnp.zeros_like(squares)
    forward(0, every[4:], 2)
    forward(0, every, 3)
    forward(1, every, 1)
    for group in range(KV_HEADS):
        settle(0, group)
        attend(0, group, 0, GROUP)
        forward(1, every[2 * group : 2 * group + 2], 2)
    queries(1)
    forward(1, every, 3)
    for group in range(KV_HEADS):
        settle(1, group)
        for half in range(2):
            attend(1, group, half * GROUP // 2, (half + 1) * GROUP // 2)
            handed(2 * group + half).start()

    for layer in range(LAYERS):
        for piece in range(PIECES):
            for step in range(1, REACH):
                hop(layer, piece, step).wait_send()
    for part in range(OUT_PARTS):
        handed(part).wait()


def per_device(hidden_in, norm_gain, self_kv, prefix_kv, partner_prefix, resp_len):
    hbm = pl.BlockSpec(memory_space=pltpu.HBM)
    bf16, f32 = jnp.bfloat16, jnp.float32
    smem = pl.BlockSpec(memory_space=pltpu.SMEM)
    large = [
        pltpu.with_memory_space_constraint(array, pltpu.HBM)
        for array in (hidden_in, norm_gain, self_kv, prefix_kv)
    ]
    return pl.pallas_call(
        kernel,
        out_shape=pltpu.VMEM((1, RESP, WIN), bf16),
        in_specs=[hbm] * 4 + [smem] * 2,
        out_specs=pl.BlockSpec(memory_space=pltpu.VMEM),
        scratch_shapes=[
            pltpu.VMEM((RESP, WIN), bf16),
            pltpu.VMEM((RESP, WIN), bf16),
            pltpu.VMEM((LAYERS, RESP, KVW), bf16),
            pltpu.VMEM((LAYERS, WIN), f32),
            pltpu.VMEM((LAYERS, PIECES, REACH, RESP, HEAD_DIM), bf16),
            pltpu.VMEM((2 * RESP, HEAD_DIM), bf16),
            pltpu.VMEM((2 * RESP, 2 * HEAD_DIM), bf16),
            pltpu.VMEM((RESP, 2 * RESP), f32),
            pltpu.VMEM((RESP, HEAD_DIM), f32),
            pltpu.SemaphoreType.DMA((3,)),
            pltpu.SemaphoreType.DMA((LAYERS, PIECES)),
            pltpu.SemaphoreType.DMA((LAYERS, PIECES, REACH - 1)),
            pltpu.SemaphoreType.DMA((LAYERS, PIECES, REACH - 1)),
            pltpu.SemaphoreType.DMA((OUT_PARTS,)),
            pltpu.SemaphoreType.DMA((OUT_PARTS,)),
        ],
        compiler_params=pltpu.CompilerParams(
            collective_id=0, has_side_effects=True, vmem_limit_bytes=48 * 2**20
        ),
        name="judge",
    )(*large, partner_prefix, resp_len)


def solution(mesh):
    return jax.shard_map(
        per_device,
        mesh=mesh,
        in_specs=(
            P("pipe", "dp", None),
            P("pipe", None, None),
            P("pipe", None, "dp", None),
            P("pipe", None, "dp", None),
            P("dp"),
            P("dp"),
        ),
        out_specs=P("pipe", "dp", None),
        check_vma=False,
    )
```

time: 122 us -> 61.8 us (0.51)
  the two profiles are of different devices: /device:TPU:24 before, /device:TPU:1 now
where the time goes in v1:
time: 61.8 us; the launch traced here: 61.6 us
  Pallas kernels  59.4 us (96%)
  between operations  1.3 us (2%)
  local copies, waits for them, and re-layouts  0.97 us (2%)
    pallas_call x1, Pallas kernels, per_device(): pl.pallas_call(kernel, out_shape=pltpu.VMEM((1, RESP, WIN), bf16), in_spe...  59.4 us

profile of v1, /device:TPU:1, one launch (start us, length us, event | category | flops | bytes accessed | tf_op | source)
XLA Modules:
  0.0 61.6 jit_solution(10000034174794380601)
XLA Ops:
  1.3 59.4 %judge.1 = bf16[1,128,4096]{2,1,0:T(8,128)(2,1)S(1)} custom-call(bf16[1,128,4096]{2,1,0:T(8,128)(2,1)} %hid_ref.1, f32[1,2,4096]{2,1,0:T(2,128)} %gain_ref.1, bf16[1,2,128,1024]{3,2,1,0:T(8,128)(2,1)} %own_ref.1, bf16[1,2,128,1024]{3,2,1,0:T(8,128)(2,1)} %pre_ref.1, s32[1]{0:T(128)S(6)} %copy.9.partner, s32[1]{0:T(128)S(6)} %copy.10.length), custom_call_target="tpu_custom_call" | custom-call | tf_op jit(solution)/shard_map/judge/pallas_call | solution.py:200
  60.7 1.0 %copy.8 = bf16[1,128,4096]{2,1,0:T(8,128)(2,1)} copy(bf16[1,128,4096]{2,1,0:T(8,128)(2,1)S(1)} %judge.1) | data formatting | bytes 2097152

commit v2 on v1

v2 whole, which is shorter than its diff:
```python
import math

import jax
import jax.numpy as jnp
from jax import lax
from jax.experimental import pallas as pl
from jax.experimental.pallas import tpu as pltpu
from jax.sharding import PartitionSpec as P

HEADS = 32
KV_HEADS = 4
GROUP = HEADS // KV_HEADS
HEAD_DIM = 128
LAYERS = 2
REACH = 4
RESP = 128
WIN = HEADS * HEAD_DIM
KVW = 2 * KV_HEADS * HEAD_DIM
HALF = KVW // 2
PIECES = 2 * KV_HEADS
SCALE = math.log2(math.e) / math.sqrt(HEAD_DIM)
OUT_PARTS = KV_HEADS
PART = WIN // OUT_PARTS
MESH = pl.DeviceIdType.MESH
DEPTH = 16
WAYS = 4
LAG = 2
HEAD_START = 5
SLOTS = [(layer, group, step) for step in range(1, REACH) for layer in range(LAYERS) for group in range(KV_HEADS)]


def kernel(hid_ref, gain_ref, own_ref, pre_ref, partner, length, out_ref,
           h, own, gain, pre, kcat, vcat, bias, squares, factor,
           way, turn, load_sem, slot_sem, send_sem, recv_sem, way_send, way_recv, out_send, out_recv):
    pipe, dp = lax.axis_index("pipe"), lax.axis_index("dp")
    sections, owners = lax.axis_size("pipe"), lax.axis_size("dp")
    right = (pipe, lax.rem(dp + 1, owners))
    left = (pipe, lax.rem(dp + owners - 1, owners))
    below = (pipe, lax.rem(dp + DEPTH, owners))
    above = (pipe, lax.rem(dp + owners - DEPTH, owners))
    start_of_row = (pipe, lax.rem(dp + owners - DEPTH + 1, owners))
    onward = (lax.rem(pipe + 1, sections), dp)
    back = (lax.rem(pipe + sections - 1, sections), dp)

    y, z = dp // DEPTH, dp % DEPTH
    low, high = z == 0, z == DEPTH - 1
    flows = high & (dp < owners - 1)
    relays = high & (y > 0)

    barrier = pltpu.get_barrier_semaphore()
    pl.semaphore_signal(barrier, inc=1, device_id=back, device_id_type=MESH)

    @pl.when(pipe % 2 == 0)
    def _():
        pl.semaphore_signal(barrier, inc=1, device_id=onward, device_id_type=MESH)

    @pl.when(dp > 0)
    def _():
        pl.semaphore_signal(barrier, inc=1, device_id=left, device_id_type=MESH)

    @pl.when(relays)
    def _():
        pl.semaphore_signal(barrier, inc=1, device_id=above, device_id_type=MESH)

    @pl.when(low & (y > 0))
    def _():
        pl.semaphore_signal(barrier, inc=1, device_id=(pipe, dp + DEPTH - 1), device_id_type=MESH)

    def column(piece):
        return (piece % 2) * HALF + (piece // 2) * HEAD_DIM

    def owned(layer, piece):
        return pre_ref.at[0, layer, :, pl.ds(column(piece), HEAD_DIM)]

    loads = [
        pltpu.make_async_copy(hid_ref.at[0], h, load_sem.at[0]),
        pltpu.make_async_copy(gain_ref.at[0], gain, load_sem.at[1]),
        pltpu.make_async_copy(own_ref.at[0], own, load_sem.at[2]),
    ]
    slots = [
        pltpu.make_async_copy(owned(layer, piece), pre.at[layer, piece, 0], slot_sem.at[layer, piece])
        for layer in range(LAYERS)
        for piece in range(PIECES)
    ]
    for copy in loads:
        copy.start()
    odd = pipe % 2 == 1
    greeted = 1 + sum(condition.astype(jnp.int32) for condition in (odd, dp < owners - 1, flows, relays))
    pl.semaphore_wait(barrier, greeted)

    def hop(layer, piece, step):
        source = owned(layer, piece) if step == 1 else pre.at[layer, piece, step - 1]
        return pltpu.make_async_remote_copy(
            src_ref=source,
            dst_ref=pre.at[layer, piece, step],
            send_sem=send_sem.at[layer, piece, step - 1],
            recv_sem=recv_sem.at[layer, piece, step - 1],
            device_id=right,
            device_id_type=MESH,
        )

    def aside(layer, piece, step):
        source = owned(layer, piece) if step == 1 else pre.at[layer, piece, step - 1]
        return pltpu.make_async_remote_copy(
            src_ref=source,
            dst_ref=way.at[layer, piece, step - 1],
            send_sem=send_sem.at[layer, piece, step - 1],
            recv_sem=way_recv.at[layer, piece, step - 1],
            device_id=below,
            device_id_type=MESH,
        )

    def relayed(layer, piece, step):
        return pltpu.make_async_remote_copy(
            src_ref=way.at[layer, piece, step - 1],
            dst_ref=pre.at[layer, piece, step],
            send_sem=way_send.at[layer, piece, step - 1],
            recv_sem=recv_sem.at[layer, piece, step - 1],
            device_id=start_of_row,
            device_id_type=MESH,
        )

    def pieces_of(group):
        return 2 * group, 2 * group + 1

    def arrive(layer, group, step):
        @pl.when(dp >= step)
        def _():
            for piece in pieces_of(group):
                hop(layer, piece, step).wait_recv()

    def forward(layer, group, step):
        if step > 1:
            arrive(layer, group, step - 1)

        @pl.when((dp >= step - 1) & (z < DEPTH - 1))
        def _():
            for piece in pieces_of(group):
                hop(layer, piece, step).start()

        @pl.when(flows)
        def _():
            for piece in pieces_of(group):
                rank = piece % WAYS

                @pl.when(y < rank)
                def _():
                    hop(layer, piece, step).start()

                if rank < WAYS - 1:

                    @pl.when(y >= rank)
                    def _():
                        aside(layer, piece, step).start()

    def relay(layer, group, step, sent=False):
        @pl.when(relays)
        def _():
            for piece in pieces_of(group):
                rank = piece % WAYS
                if rank < WAYS - 1:

                    @pl.when(y > rank)
                    def _():
                        if sent:
                            relayed(layer, piece, step).wait_send()
                        else:
                            aside(layer, piece, step).wait_recv()
                            relayed(layer, piece, step).start()

    def sent(layer, group, step):
        early = step == 1 and (layer, group, step) in SLOTS[:HEAD_START]
        @pl.when((dp >= step - 1) & (dp < owners - 1) & (jnp.logical_not(odd) if early else True))
        def _():
            for piece in pieces_of(group):
                hop(layer, piece, step).wait_send()

    def handed(part):
        columns = pl.ds(part * PART, PART)
        return pltpu.make_async_remote_copy(
            src_ref=h.at[:, columns],
            dst_ref=out_ref.at[0, :, columns],
            send_sem=out_send.at[part],
            recv_sem=out_recv.at[part],
            device_id=onward,
            device_id_type=MESH,
        )

    def head_columns(head):
        return pl.ds(pl.multiple_of(head * HEAD_DIM, HEAD_DIM), HEAD_DIM)

    def add_squares():
        squares[...] = jnp.zeros_like(squares)

        @pl.loop(0, HEADS // GROUP)
        def _(group):
            summed = squares[...]
            for within in range(GROUP):
                x = h[:, head_columns(group * GROUP + within)].astype(jnp.float32)
                summed = summed + x * x
            squares[...] = summed

    def settle_norm():
        mean = jnp.sum(squares[...], axis=-1, keepdims=True) * (1.0 / WIN)
        factor[...] = jnp.broadcast_to(lax.rsqrt(mean + 1e-05), (RESP, HEAD_DIM))

    def chosen(layer, piece):
        offset = dp - partner[0]
        block = pre[layer, piece, 0]
        for step in range(1, REACH):
            block = jnp.where(offset == step, pre[layer, piece, step], block)
        return block

    def mix(layer, columns):
        x = h[:, columns].astype(jnp.float32)
        query = (x * factor[...] * gain[pl.ds(layer, 1), columns]).astype(jnp.bfloat16)
        scores = lax.dot_general(
            query, kcat[...], (((1,), (1,)), ((), ())), preferred_element_type=jnp.float32
        )
        scores = scores * SCALE + bias[...]
        top = jnp.max(scores, axis=-1, keepdims=True)
        expo = jnp.exp2(scores - top).astype(jnp.bfloat16)
        mixed = jnp.dot(expo, vcat[...], preferred_element_type=jnp.float32)
        return (x + mixed[:, :HEAD_DIM] / mixed[:, HEAD_DIM:]).astype(jnp.bfloat16)

    def attend(layer, group):
        heads = [pl.ds((group * GROUP + within) * HEAD_DIM, HEAD_DIM) for within in range(GROUP)]
        totals = [mix(layer, columns) for columns in heads]
        for columns, total in zip(heads, totals):
            h[:, columns] = total
        if layer + 1 < LAYERS:
            summed = squares[...]
            for total in totals:
                x = total.astype(jnp.float32)
                summed = summed + x * x
            squares[...] = summed

    def settle(layer, group):
        arrive(layer, group, REACH - 1)
        for piece in pieces_of(group):
            slots[layer * PIECES + piece].wait()
        kcat[pl.ds(0, RESP), :] = chosen(layer, 2 * group)
        kcat[pl.ds(RESP, RESP), :] = own[layer, :, pl.ds(group * HEAD_DIM, HEAD_DIM)]
        vcat[pl.ds(0, RESP), pl.ds(0, HEAD_DIM)] = chosen(layer, 2 * group + 1)
        vcat[pl.ds(RESP, RESP), pl.ds(0, HEAD_DIM)] = own[layer, :, pl.ds(HALF + group * HEAD_DIM, HEAD_DIM)]

    def prepare():
        for copy in slots:
            copy.start()
        vcat[:, pl.ds(HEAD_DIM, HEAD_DIM)] = jnp.ones((2 * RESP, HEAD_DIM), jnp.bfloat16)
        for copy in loads:
            copy.wait()
        row = lax.broadcasted_iota(jnp.int32, (RESP, RESP), 0)
        key = lax.broadcasted_iota(jnp.int32, (RESP, RESP), 1)
        seen = (key <= row) & (key < length[0])
        bias[:, pl.ds(0, RESP)] = jnp.zeros((RESP, RESP), jnp.float32)
        bias[:, pl.ds(RESP, RESP)] = jnp.where(seen, 0.0, -1e30)
        add_squares()
        settle_norm()
        squares[...] = jnp.zeros_like(squares)

    def first(group):
        settle(0, group)
        attend(0, group)
        if group == KV_HEADS - 1:
            settle_norm()

    def second(group):
        settle(1, group)
        attend(1, group)
        handed(group).start()

    @pl.when(jnp.logical_not(odd) & (dp < owners - 1))
    def _():
        pl.semaphore_wait(turn, 1)

    for index, (layer, group, step) in enumerate(SLOTS):
        forward(layer, group, step)
        if index == 7:
            @pl.when(odd & (dp < owners - 1))
            def _():
                for slot in SLOTS[:HEAD_START]:
                    for piece in pieces_of(slot[1]):
                        hop(slot[0], piece, 1).wait_send()
                pl.semaphore_signal(turn, inc=1, device_id=back, device_id_type=MESH)
        if index == 7:
            prepare()
        if index >= LAG:
            relay(*SLOTS[index - LAG])
    for slot in SLOTS[len(SLOTS) - LAG :]:
        relay(*slot)
    for group in range(KV_HEADS):
        first(group)
    for group in range(KV_HEADS):
        second(group)

    for slot in SLOTS:
        sent(*slot)
        relay(*slot, sent=True)
    for part in range(OUT_PARTS):
        handed(part).wait()


def per_device(hidden_in, norm_gain, self_kv, prefix_kv, partner_prefix, resp_len):
    hbm = pl.BlockSpec(memory_space=pltpu.HBM)
    bf16, f32 = jnp.bfloat16, jnp.float32
    smem = pl.BlockSpec(memory_space=pltpu.SMEM)
    large = [
        pltpu.with_memory_space_constraint(array, pltpu.HBM)
        for array in (hidden_in, norm_gain, self_kv, prefix_kv)
    ]
    return pl.pallas_call(
        kernel,
        out_shape=pltpu.VMEM((1, RESP, WIN), bf16),
        in_specs=[hbm] * 4 + [smem] * 2,
        out_specs=pl.BlockSpec(memory_space=pltpu.VMEM),
        scratch_shapes=[
            pltpu.VMEM((RESP, WIN), bf16),
            pltpu.VMEM((LAYERS, RESP, KVW), bf16),
            pltpu.VMEM((LAYERS, WIN), f32),
            pltpu.VMEM((LAYERS, PIECES, REACH, RESP, HEAD_DIM), bf16),
            pltpu.VMEM((2 * RESP, HEAD_DIM), bf16),
            pltpu.VMEM((2 * RESP, 2 * HEAD_DIM), bf16),
            pltpu.VMEM((RESP, 2 * RESP), f32),
            pltpu.VMEM((RESP, HEAD_DIM), f32),
            pltpu.VMEM((RESP, HEAD_DIM), f32),
            pltpu.VMEM((LAYERS, PIECES, REACH - 1, RESP, HEAD_DIM), bf16),
            pltpu.SemaphoreType.REGULAR,
            pltpu.SemaphoreType.DMA((3,)),
            pltpu.SemaphoreType.DMA((LAYERS, PIECES)),
            pltpu.SemaphoreType.DMA((LAYERS, PIECES, REACH - 1)),
            pltpu.SemaphoreType.DMA((LAYERS, PIECES, REACH - 1)),
            pltpu.SemaphoreType.DMA((LAYERS, PIECES, REACH - 1)),
            pltpu.SemaphoreType.DMA((LAYERS, PIECES, REACH - 1)),
            pltpu.SemaphoreType.DMA((OUT_PARTS,)),
            pltpu.SemaphoreType.DMA((OUT_PARTS,)),
        ],
        compiler_params=pltpu.CompilerParams(
            collective_id=0, has_side_effects=True, vmem_limit_bytes=48 * 2**20
        ),
        name="judge",
    )(*large, partner_prefix, resp_len)


def solution(mesh):
    return jax.shard_map(
        per_device,
        mesh=mesh,
        in_specs=(
            P("pipe", "dp", None),
            P("pipe", None, None),
            P("pipe", None, "dp", None),
            P("pipe", None, "dp", None),
            P("dp"),
            P("dp"),
        ),
        out_specs=P("pipe", "dp", None),
        check_vma=False,
    )
```

time: 61.8 us -> 52.7 us (0.85)
  the two profiles are of different devices: /device:TPU:1 before, /device:TPU:24 now
where the time goes in v2:
time: 52.7 us; the launch traced here: 52.4 us
  Pallas kernels  50.1 us (95%)
  between operations  1.3 us (2%)
  local copies, waits for them, and re-layouts  0.97 us (2%)
    pallas_call x1, Pallas kernels, per_device(): pl.pallas_call(kernel, out_shape=pltpu.VMEM((1, RESP, WIN), bf16), in_spe...  50.1 us

profile of v2, /device:TPU:24, one launch (start us, length us, event | category | flops | bytes accessed | tf_op | source)
XLA Modules:
  0.0 52.4 jit_solution(8165692141221675173)
XLA Ops:
  1.3 50.1 %judge.1 = bf16[1,128,4096]{2,1,0:T(8,128)(2,1)S(1)} custom-call(bf16[1,128,4096]{2,1,0:T(8,128)(2,1)} %hid_ref.1, f32[1,2,4096]{2,1,0:T(2,128)} %gain_ref.1, bf16[1,2,128,1024]{3,2,1,0:T(8,128)(2,1)} %own_ref.1, bf16[1,2,128,1024]{3,2,1,0:T(8,128)(2,1)} %pre_ref.1, s32[1]{0:T(128)S(6)} %copy.9.partner, s32[1]{0:T(128)S(6)} %copy.10.length), custom_call_target="tpu_custom_call" | custom-call | tf_op jit(solution)/shard_map/judge/pallas_call | solution.py:312
  51.4 1.0 %copy.8 = bf16[1,128,4096]{2,1,0:T(8,128)(2,1)} copy(bf16[1,128,4096]{2,1,0:T(8,128)(2,1)S(1)} %judge.1) | data formatting | bytes 2097152

commit v3 on v2

--- a/solution.py
+++ b/solution.py
@@ -31,7 +31,7 @@
 
 def kernel(hid_ref, gain_ref, own_ref, pre_ref, partner, length, out_ref,
            h, own, gain, pre, kcat, vcat, bias, squares, factor,
-           way, turn, load_sem, slot_sem, send_sem, recv_sem, way_send, way_recv, out_send, out_recv):
+           way, turn, ready, load_sem, slot_sem, send_sem, recv_sem, way_send, way_recv, out_send, out_recv):
     pipe, dp = lax.axis_index("pipe"), lax.axis_index("dp")
     sections, owners = lax.axis_size("pipe"), lax.axis_size("dp")
     right = (pipe, lax.rem(dp + 1, owners))
@@ -48,11 +48,13 @@
     relays = high & (y > 0)
 
     barrier = pltpu.get_barrier_semaphore()
-    pl.semaphore_signal(barrier, inc=1, device_id=back, device_id_type=MESH)
-
-    @pl.when(pipe % 2 == 0)
-    def _():
-        pl.semaphore_signal(barrier, inc=1, device_id=onward, device_id_type=MESH)
+    odd = pipe % 2 == 1
+    even = jnp.logical_not(odd)
+    pl.semaphore_signal(barrier, inc=1, device_id=onward, device_id_type=MESH)
+
+    @pl.when(odd)
+    def _():
+        pl.semaphore_signal(barrier, inc=1, device_id=back, device_id_type=MESH)
 
     @pl.when(dp > 0)
     def _():
@@ -84,9 +86,12 @@
     ]
     for copy in loads:
         copy.start()
-    odd = pipe % 2 == 1
-    greeted = 1 + sum(condition.astype(jnp.int32) for condition in (odd, dp < owners - 1, flows, relays))
+    greeted = 1 + sum(condition.astype(jnp.int32) for condition in (even, dp < owners - 1, flows, relays))
     pl.semaphore_wait(barrier, greeted)
+
+    @pl.when(even)
+    def _():
+        pl.semaphore_signal(ready, inc=1, device_id=back, device_id_type=MESH)
 
     def hop(layer, piece, step):
         source = owned(layer, piece) if step == 1 else pre.at[layer, piece, step - 1]
@@ -270,7 +275,7 @@
         attend(1, group)
         handed(group).start()
 
-    @pl.when(jnp.logical_not(odd) & (dp < owners - 1))
+    @pl.when(even & (dp < owners - 1))
     def _():
         pl.semaphore_wait(turn, 1)
 
@@ -291,6 +296,11 @@
         relay(*slot)
     for group in range(KV_HEADS):
         first(group)
+
+    @pl.when(odd)
+    def _():
+        pl.semaphore_wait(ready, 1)
+
     for group in range(KV_HEADS):
         second(group)
 
@@ -326,6 +336,7 @@
             pltpu.VMEM((RESP, HEAD_DIM), f32),
             pltpu.VMEM((LAYERS, PIECES, REACH - 1, RESP, HEAD_DIM), bf16),
             pltpu.SemaphoreType.REGULAR,
+            pltpu.SemaphoreType.REGULAR,
             pltpu.SemaphoreType.DMA((3,)),
             pltpu.SemaphoreType.DMA((LAYERS, PIECES)),
             pltpu.SemaphoreType.DMA((LAYERS, PIECES, REACH - 1)),

time: 52.7 us -> 52.5 us (level)
  no operation moved by 1% of the time
where the time goes in v3:
time: 52.5 us; the launch traced here: 52.4 us
  Pallas kernels  50.1 us (95%)
  between operations  1.3 us (2%)
  local copies, waits for them, and re-layouts  0.97 us (2%)
    pallas_call x1, Pallas kernels, per_device(): pl.pallas_call(kernel, out_shape=pltpu.VMEM((1, RESP, WIN), bf16), in_spe...  50.1 us

profile of v3, /device:TPU:24, one launch (start us, length us, event | category | flops | bytes accessed | tf_op | source)
XLA Modules:
  0.0 52.4 jit_solution(5730352345523849522)
XLA Ops:
  1.3 50.1 %judge.1 = bf16[1,128,4096]{2,1,0:T(8,128)(2,1)S(1)} custom-call(bf16[1,128,4096]{2,1,0:T(8,128)(2,1)} %hid_ref.1, f32[1,2,4096]{2,1,0:T(2,128)} %gain_ref.1, bf16[1,2,128,1024]{3,2,1,0:T(8,128)(2,1)} %own_ref.1, bf16[1,2,128,1024]{3,2,1,0:T(8,128)(2,1)} %pre_ref.1, s32[1]{0:T(128)S(6)} %copy.9.partner, s32[1]{0:T(128)S(6)} %copy.10.length), custom_call_target="tpu_custom_call" | custom-call | tf_op jit(solution)/shard_map/judge/pallas_call | solution.py:322
  51.4 1.0 %copy.8 = bf16[1,128,4096]{2,1,0:T(8,128)(2,1)} copy(bf16[1,128,4096]{2,1,0:T(8,128)(2,1)S(1)} %judge.1) | data formatting | bytes 2097152

commit v4 on v3

--- a/solution.py
+++ b/solution.py
@@ -19,7 +19,7 @@
 HALF = KVW // 2
 PIECES = 2 * KV_HEADS
 SCALE = math.log2(math.e) / math.sqrt(HEAD_DIM)
-OUT_PARTS = KV_HEADS
+OUT_PARTS = 2 * KV_HEADS
 PART = WIN // OUT_PARTS
 MESH = pl.DeviceIdType.MESH
 DEPTH = 16
@@ -228,8 +228,8 @@
         mixed = jnp.dot(expo, vcat[...], preferred_element_type=jnp.float32)
         return (x + mixed[:, :HEAD_DIM] / mixed[:, HEAD_DIM:]).astype(jnp.bfloat16)
 
-    def attend(layer, group):
-        heads = [pl.ds((group * GROUP + within) * HEAD_DIM, HEAD_DIM) for within in range(GROUP)]
+    def attend(layer, group, first=0, last=GROUP):
+        heads = [pl.ds((group * GROUP + within) * HEAD_DIM, HEAD_DIM) for within in range(first, last)]
         totals = [mix(layer, columns) for columns in heads]
         for columns, total in zip(heads, totals):
             h[:, columns] = total
@@ -272,8 +272,11 @@
 
     def second(group):
         settle(1, group)
-        attend(1, group)
-        handed(group).start()
+        pace = GROUP // 2 if group == KV_HEADS - 1 else GROUP
+        for begin in range(0, GROUP, pace):
+            attend(1, group, begin, begin + pace)
+            for head in range(begin, begin + pace, GROUP // 2):
+                handed((group * GROUP + head) * OUT_PARTS // HEADS).start()
 
     @pl.when(even & (dp < owners - 1))
     def _():

time: 52.5 us -> 52.6 us (level)
  no operation moved by 1% of the time
where the time goes in v4:
time: 52.6 us; the launch traced here: 52.4 us
  Pallas kernels  50.2 us (95%)
  between operations  1.3 us (2%)
  local copies, waits for them, and re-layouts  0.97 us (2%)
    pallas_call x1, Pallas kernels, per_device(): pl.pallas_call(kernel, out_shape=pltpu.VMEM((1, RESP, WIN), bf16), in_spe...  50.2 us

profile of v4, /device:TPU:24, one launch (start us, length us, event | category | flops | bytes accessed | tf_op | source)
XLA Modules:
  0.0 52.4 jit_solution(1101010926294311689)
XLA Ops:
  1.3 50.2 %judge.1 = bf16[1,128,4096]{2,1,0:T(8,128)(2,1)S(1)} custom-call(bf16[1,128,4096]{2,1,0:T(8,128)(2,1)} %hid_ref.1, f32[1,2,4096]{2,1,0:T(2,128)} %gain_ref.1, bf16[1,2,128,1024]{3,2,1,0:T(8,128)(2,1)} %own_ref.1, bf16[1,2,128,1024]{3,2,1,0:T(8,128)(2,1)} %pre_ref.1, s32[1]{0:T(128)S(6)} %copy.9.partner, s32[1]{0:T(128)S(6)} %copy.10.length), custom_call_target="tpu_custom_call" | custom-call | tf_op jit(solution)/shard_map/judge/pallas_call | solution.py:325
  51.5 1.0 %copy.8 = bf16[1,128,4096]{2,1,0:T(8,128)(2,1)} copy(bf16[1,128,4096]{2,1,0:T(8,128)(2,1)S(1)} %judge.1) | data formatting | bytes 2097152
